TPU v7x, 32 devices: a whole 2x2x4 slice. The times are simulated.
32 devices in a mesh: prow: 4 (over z), pcol: 8 (over y, x, core).
Axes of the slice: x: 2, y: 2, z: 4, core: 2. Of those that a mesh axis runs over, the one named last changes fastest.
Arguments:
- left_vecs: bfloat16 [16384, 4096], P(('prow', 'pcol'))
- right_vecs: bfloat16 [16384, 4096], P(('prow', 'pcol'))
- primal: bfloat16 [4096, 4096], P(('prow', 'pcol'))
- dual_inverse: bfloat16 [4096, 4096], P(('prow', 'pcol'))
- owner_map: int32 [32], replicated, may hold values from 0 to 31, each once
- panel_index: int32 [1], replicated, may hold values from 0 to 62
Outputs:
- panel_factor: float32 [256, 16384], P('pcol', 'prow')
- ahead_update: float32 [256, 16384], P('pcol', 'prow')
All inputs are finite; a program needn't handle non-finite values.
Results may differ from a plain program's by a relative error of at most 0.00067.
Values may be sent and summed in bfloat16 or wider, within the bound.
A program may use at most 128 MiB of HBM per device.

v0:
```python
import jax
import jax.numpy as jnp
from jax import lax
from jax.sharding import PartitionSpec as P

PANEL = 256


def combine(left_prod, right_prod):
    seg = 2 * PANEL
    return (
        left_prod[:, seg : 2 * seg] * right_prod[:, 2 * seg : 3 * seg]
        + right_prod[:, seg : 2 * seg] * left_prod[:, 2 * seg : 3 * seg]
        + left_prod[:, 0:seg] * right_prod[:, 3 * seg : 4 * seg]
        + right_prod[:, 0:seg] * left_prod[:, 3 * seg : 4 * seg]
    )


def relay_rows(first_part, second_part, owner_map, devices, grid_rows):
    slots = first_part.shape[0]
    height = PANEL // devices
    groups = slots // (grid_rows * height)
    grid_cols = devices // grid_rows
    narrow = PANEL // grid_cols
    stacked = jnp.stack([first_part, second_part], axis=1)
    stacked = stacked.reshape(groups, grid_rows, height, 2, grid_cols, narrow)
    outgoing = stacked.transpose(1, 4, 3, 5, 0, 2).reshape(devices, 2, narrow, groups * height)
    arrived = lax.all_to_all(outgoing, ("prow", "pcol"), split_axis=0, concat_axis=0, tiled=True)
    flat = arrived.transpose(1, 2, 0, 3).reshape(2, narrow, devices * groups * height)
    local_rows = slots * devices // grid_rows
    place = jnp.arange(local_rows, dtype=jnp.int32)
    block_num = place // PANEL
    within = place % PANEL
    index = (
        jnp.take(owner_map, within % devices) * (groups * height)
        + block_num * height
        + within // devices
    )
    placed = jnp.take(flat, index, axis=2)
    return (placed[0], placed[1])


def body(left_vecs, right_vecs, primal, dual_inverse, owner_map, panel_index):
    devices = lax.axis_size(("prow", "pcol"))
    grid_rows = lax.axis_size("prow")
    grid_cols = lax.axis_size("pcol")
    per_device = 2 * PANEL // devices
    start = panel_index[0] * PANEL
    first_slot = start // devices
    panel_left = lax.dynamic_slice_in_dim(left_vecs, first_slot, per_device, 0)
    panel_right = lax.dynamic_slice_in_dim(right_vecs, first_slot, per_device, 0)
    panel_pairs = jnp.stack([panel_left, panel_right], axis=1)
    matrices = jnp.stack([primal, dual_inverse], axis=0)
    raw_images = jnp.einsum(
        "gfn,mcn->gfmc",
        matrices,
        lax.all_gather(panel_pairs, ("prow", "pcol"), axis=0, tiled=True),
        preferred_element_type=jnp.float32,
    )
    column_ids = jnp.arange(2 * PANEL, dtype=jnp.int32)
    gathered_ids = jnp.take(owner_map, column_ids % devices) * per_device + column_ids // devices
    ordered = jnp.take(raw_images, gathered_ids, axis=2)
    feature_rows = ordered.shape[1]
    images = ordered.transpose(1, 0, 3, 2).reshape(feature_rows, 8 * PANEL).astype(jnp.bfloat16)
    piece = lax.all_gather(images, ("prow", "pcol"), axis=0, tiled=True)
    left_prod = jnp.dot(left_vecs, piece, preferred_element_type=jnp.float32)
    right_prod = jnp.dot(right_vecs, piece, preferred_element_type=jnp.float32)
    schur = combine(left_prod, right_prod)
    own_panel = lax.dynamic_slice_in_dim(schur, first_slot, per_device, 0)
    panel_block = lax.all_gather(own_panel, ("prow", "pcol"), axis=0, tiled=True)
    panel_block = jnp.take(panel_block, gathered_ids, axis=0)
    chol = jnp.linalg.cholesky(panel_block[:PANEL, :PANEL])
    inverse = lax.linalg.triangular_solve(
        chol, jnp.eye(PANEL, dtype=jnp.float32), left_side=True, lower=True
    )
    ahead = jnp.dot(
        panel_block[PANEL:, :PANEL],
        inverse.T,
        precision=lax.Precision.HIGHEST,
        preferred_element_type=jnp.float32,
    )
    first_cols, second_cols = relay_rows(
        schur[:, :PANEL], schur[:, PANEL:], owner_map, devices, grid_rows
    )
    narrow = PANEL // grid_cols
    my_col = lax.axis_index("pcol")
    through = jnp.dot(
        ahead, inverse, precision=lax.Precision.HIGHEST, preferred_element_type=jnp.float32
    )
    coefficient = jnp.concatenate(
        [
            lax.dynamic_slice_in_dim(inverse, my_col * narrow, narrow, 0),
            lax.dynamic_slice_in_dim(through, my_col * narrow, narrow, 0),
        ],
        axis=0,
    )
    mixed = jnp.dot(
        coefficient,
        lax.all_gather(first_cols, "pcol", axis=0, tiled=True),
        precision=lax.Precision.HIGHEST,
        preferred_element_type=jnp.float32,
    )
    local_rows = first_cols.shape[1]
    place = jnp.arange(local_rows, dtype=jnp.int32)
    schur_ids = (place // PANEL * grid_rows + lax.axis_index("prow")) * PANEL + place % PANEL
    factor_out = jnp.where((schur_ids >= start)[None, :], mixed[:narrow], jnp.float32(0.0))
    update_out = jnp.where(
        (schur_ids >= start + PANEL)[None, :], second_cols - mixed[narrow:], jnp.float32(0.0)
    )
    return (factor_out, update_out)


def solution(mesh):
    return jax.shard_map(
        body,
        mesh=mesh,
        in_specs=(
            P(("prow", "pcol"), None),
            P(("prow", "pcol"), None),
            P(("prow", "pcol"), None),
            P(("prow", "pcol"), None),
            P(),
            P(),
        ),
        out_specs=(P("pcol", "prow"), P("pcol", "prow")),
        check_vma=False,
    )
```

profile of v0, /device:TPU:0, one launch (start us, length us, event | category | flops | bytes accessed | tf_op | source)
XLA Modules:
  0.0 446.7 jit_solution(6536282702127739829)
XLA Ops:
  10.2 1.8 fusion.64
  12.0 4.3 compare_select_fusion.15
  16.3 2.1 fusion.63
  18.4 15.6 %compare_and_fusion.1 = (pred[512]{0:T(512)(128)(4,1)S(1)}, s32[512]{0:T(512)S(1)}) fusion(pred[512]{0:T(512)(128)(4,1)S(1)} %get-tuple-element.66, pred[512]{0:T(512)(128)(4,1)S(1)} %get-tuple-element.67, pred[512]{0:T(512)(128)(4,1)S(1)} %get-tuple-element.68, pred[512]{0:T(512)(128)(4,1)S(1)} %get-tuple-element.69, ...), kind=kLoop, calls=%fused_computation.203 | loop fusion | flops 26624 | bytes 17508 | tf_op jit(solution)/shard_map/jit(_take)/and | solution.py:71
  34.1 57.5 %all-gather.6.cloned.1.call-done = bf16[512,2,4096]{2,0,1:T(8,128)(2,1)} async-done(((bf16[16,2,4096]{2,0,1:T(8,128)(2,1)}), bf16[512,2,4096]{2,0,1:T(8,128)(2,1)}) %all-gather.6.cloned.1.call-update) | async-done | bytes 8388624 | tf_op jit(solution)/shard_map/all_gather | solution.py:57
  91.6 6.4 %fusion = bf16[2,128,512,2]{2,1,3,0:T(8,128)(2,1)S(1)} fusion(bf16[512,2,4096]{2,0,1:T(8,128)(2,1)} %all-gather.6.cloned.1.call-done, bf16[1,128,4096]{2,1,0:T(8,128)(2,1)} %bitcast.120, bf16[1,128,4096]{2,1,0:T(8,128)(2,1)} %bitcast.121), kind=kOutput, calls=%fused_computation.5 | convolution fusion | flops 2151677952 | bytes 11010048 | tf_op jit(solution)/shard_map/gfn,mcn->gfmc/dot_general | solution.py:54
  98.4 2.3 gather_fusion
  100.7 1.8 fusion.10
  105.5 144.0 %all-gather.8.cloned.1.call-done = bf16[4096,2048]{0,1:T(8,128)(2,1)} async-done(((bf16[128,2048]{0,1:T(8,128)(2,1)}), bf16[4096,2048]{0,1:T(8,128)(2,1)}) %all-gather.8.cloned.1.call-update) | async-done | bytes 16777232 | tf_op jit(solution)/shard_map/all_gather | solution.py:65
  249.4 13.1 %convolution_bitcast_fusion = f32[512,2048]{1,0:T(8,128)S(1)} fusion(bf16[4096,2048]{0,1:T(8,128)(2,1)} %all-gather.8.cloned.1.call-done, bf16[512,4096]{1,0:T(8,128)(2,1)} %param.7), kind=kOutput, calls=%fused_computation.10 | convolution fusion | flops 8589934592 | bytes 25165824 | tf_op jit(solution)/shard_map/dot_general | solution.py:67
  262.5 11.7 %convolution_bitcast_fusion.1 = f32[512,2048]{1,0:T(8,128)S(1)} fusion(bf16[4096,2048]{0,1:T(8,128)(2,1)} %all-gather.8.cloned.1.call-done, bf16[512,4096]{1,0:T(8,128)(2,1)S(1)} %copy-done.1), kind=kOutput, calls=%fused_computation.11 | convolution fusion | flops 8589934592 | bytes 25165824 | tf_op jit(solution)/shard_map/dot_general | solution.py:66
  276.3 1.6 stack.33
  277.9 1.7 copy.23
  279.6 1.6 stack.34
  282.8 2.3 pad_maximum_fusion
  285.1 3.6 copy.25
  288.7 2.8 all-to-all-start
  292.1 4.4 compare_select_fusion.2
  296.5 15.7 %compare_and_fusion = (pred[4096]{0:T(1024)(128)(4,1)S(1)}, s32[4096]{0:T(1024)S(1)}) fusion(pred[4096]{0:T(1024)(128)(4,1)S(1)} %compare_reduce_fusion, pred[4096]{0:T(1024)(128)(4,1)S(1)} %compare_reduce_fusion.1, pred[4096]{0:T(1024)(128)(4,1)S(1)} %compare_reduce_fusion.2, pred[4096]{0:T(1024)(128)(4,1)S(1)} %compare_reduce_fusion.3, ...), kind=kLoop, calls=%fused_computation.141 | loop fusion | flops 299008 | bytes 139364 | tf_op jit(solution)/shard_map/jit(_take)/and | solution.py:39
  312.9 4.8 %all-to-all-done = f32[32,2,32,128]{3,2,1,0:T(8,128)S(1)} async-done(((f32[32,2,32,128]{3,2,1,0:T(8,128)}), f32[32,2,32,128]{3,2,1,0:T(8,128)S(1)}, u32[]{:S(2)}, u32[]{:S(2)}) %all-to-all-start) | async-done | bytes 1048608 | tf_op jit(solution)/shard_map/all_to_all | solution.py:28
  317.7 4.3 copy.30
  322.0 30.5 %gather_fusion.2 = f32[4096,2,32]{2,1,0:T(2,128)} fusion(f32[2,32,4096]{1,0,2:T(2,128)} %bitcast.111, s32[4096]{0:T(1024)S(1)} %broadcast_clamp_fusion), kind=kCustom, calls=%fused_computation.2 | custom fusion | bytes 2113536 | tf_op jit(solution)/shard_map/jit(_take)/gather | solution.py:39
  352.5 5.2 %copy.28 = f32[4096,2,32]{0,2,1:T(8,128)S(1)} copy(f32[4096,2,32]{2,1,0:T(2,128)} %gather_fusion.2) | data formatting | bytes 2097152 | tf_op jit(solution)/shard_map/jit(_take)/gather | solution.py:39
  358.8 9.0 %all-gather.10.cloned.1.call-done = f32[512,512]{1,0:T(8,128)} async-done(((f32[16,512]{1,0:T(8,128)}), f32[512,512]{1,0:T(8,128)}) %all-gather.10.cloned.1.call-update) | async-done | bytes 1048592 | tf_op jit(solution)/shard_map/all_gather | solution.py:70
  367.8 3.5 gather_fusion.1
  372.0 11.7 %cholesky.50 = f32[128,128]{1,0:T(8,128)S(1)} custom-call(f32[128,128]{1,0:T(8,128)S(1)} %cholesky.118), custom_call_target="Cholesky" | custom-call | tf_op jit(solution)/shard_map/jit(cholesky)/cholesky | solution.py:72
  383.8 9.8 %custom-call.14 = f32[1,128,128]{1,2,0:T(8,128)S(1)} custom-call(f32[1,128,128]{2,1,0:T(8,128)S(1)} %get-tuple-element.31), custom_call_target="InvertDiagBlocksLowerTriangular" | custom-call | tf_op jit(solution)/shard_map/jit(cholesky)/cholesky | solution.py:72
  394.1 11.7 %cholesky.105 = f32[128,128]{1,0:T(8,128)S(1)} custom-call(f32[128,128]{1,0:T(8,128)S(1)} %convolution_subtract_fusion.1), custom_call_target="Cholesky" | custom-call | tf_op jit(solution)/shard_map/jit(cholesky)/cholesky | solution.py:72
  408.5 3.9 while.1
  409.1 1.4 bitcast_dynamic-update-slice_fusion.2
  412.4 19.9 %custom-call.15 = f32[2,128,128]{1,2,0:T(8,128)S(1)} custom-call(f32[2,128,128]{2,1,0:T(8,128)S(1)} %get-tuple-element.9), custom_call_target="InvertDiagBlocksLowerTriangular" | custom-call | tf_op jit(solution)/shard_map/triangular_solve | solution.py:73
  434.3 4.8 %fusion.2 = f32[64,4096]{1,0:T(8,128)S(1)} fusion(f32[1,256,4096]{2,1,0:T(8,128)} %all-gather.12.cloned.1.call-done, f32[32,256]{1,0:T(8,128)S(1)} %constant_dynamic-slice_fusion.1, f32[32,256]{1,0:T(8,128)S(1)} %fusion.25), kind=kOutput, calls=%fused_computation.8 | convolution fusion | flops 805322752 | bytes 5308416 | tf_op jit(solution)/shard_map/dot_general | solution.py:97
  (97 shorter events, 19.7 us)
Async XLA Ops:
  7.2 84.4 %all-gather.6.cloned.1.call-start = ((), (), s32[]{:S(2)}) async-start(), calls=%async_computation.1 | async-start | bytes 8650752 | tf_op jit(solution)/shard_map/all_gather | solution.py:57
  9.7 239.7 %all-gather.8.cloned.1.call-start = ((), (), s32[]{:S(2)}) async-start(), calls=%async_computation.2 | async-start | bytes 17301504 | tf_op jit(solution)/shard_map/all_gather | solution.py:65
  249.4 13.1 %copy-start.1 = (bf16[512,4096]{1,0:T(8,128)(2,1)S(1)}, bf16[512,4096]{1,0:T(8,128)(2,1)}, u32[]{:S(2)}) copy-start(bf16[512,4096]{1,0:T(8,128)(2,1)} %param.6) | copy-start | bytes 12582916
  281.2 1.6 copy-start
  288.7 29.0 %all-to-all-start = ((f32[32,2,32,128]{3,2,1,0:T(8,128)}), f32[32,2,32,128]{3,2,1,0:T(8,128)S(1)}, u32[]{:S(2)}, u32[]{:S(2)}) async-start(f32[32,2,32,128]{3,2,1,0:T(8,128)} %copy.25), calls=%async_computation | async-start | bytes 2097152 | tf_op jit(solution)/shard_map/all_to_all | solution.py:28
  291.5 76.4 %all-gather.10.cloned.1.call-start = ((), (), s32[]{:S(2)}) async-start(), calls=%async_computation.3 | async-start | bytes 1081344 | tf_op jit(solution)/shard_map/all_gather | solution.py:70
  312.8 121.5 %all-gather.12.cloned.1.call-start = ((), (), s32[]{:S(2)}) async-start(), calls=%async_computation.4 | async-start | bytes 4718592 | tf_op jit(solution)/shard_map/all_gather | solution.py:99
Sparse Core Ops, SparseCore 0:
  11.5 80.0 all-gather.5
  103.5 145.8 all-gather.7
  312.9 54.8 all-gather.9
  370.2 35.9 all-gather.11
where the time goes:
time: 448 us; the launch traced here: 447 us
  waiting for transfers between devices  215 us (48%)
  other arithmetic  105 us (23%)
  local copies, waits for them, and re-layouts  69.2 us (15%)
  matrix products  38.2 us (9%)
  between operations  16.1 us (4%)
    all_gather x1, waiting for transfers between devices, body(): piece = lax.all_gather(images, ('prow', 'pcol'), axis=0, tiled=True)  144 us
    all_gather x1, waiting for transfers between devices, body(): lax.all_gather(panel_pairs, ('prow', 'pcol'), axis=0, tiled=True)  57.5 us
    gather x2, local copies, waits for them, and re-layouts, relay_rows(): placed = jnp.take(flat, index, axis=2)  35.7 us
    another operation x7, other arithmetic, body(): chol = jnp.linalg.cholesky(panel_block[:PANEL, :PANEL])  34.6 us
    another operation x4, other arithmetic, body(): lax.linalg.triangular_solve(chol, jnp.eye(PANEL, dtype=jnp.float32), left...  20 us
    and x1, other arithmetic, relay_rows(): placed = jnp.take(flat, index, axis=2)  15.7 us
    and x1, other arithmetic, body(): panel_block = jnp.take(panel_block, gathered_ids, axis=0)  15.6 us
    dot_general x1, matrix products, body(): right_prod = jnp.dot(right_vecs, piece, preferred_element_type=jnp.float32)  13.1 us
  transfers between devices with their start and end apart: 5, of which 4 were waited for; matrix products, arithmetic and copies ran while one was open for 34% of the time, Pallas kernels for 0%

commit v1 on v0

v1 whole, which is shorter than its diff:
```python
import jax
import jax.numpy as jnp
from jax import lax
from jax.experimental import pallas as pl
from jax.experimental.pallas import tpu as pltpu
from jax.sharding import PartitionSpec as P

PANEL = 256
BLOCK = 64
HIGH = lax.Precision.HIGHEST
F32 = jnp.float32


def combine(left_prod, right_prod):
    seg = left_prod.shape[1] // 4
    return (
        left_prod[:, seg : 2 * seg] * right_prod[:, 2 * seg : 3 * seg]
        + right_prod[:, seg : 2 * seg] * left_prod[:, 2 * seg : 3 * seg]
        + left_prod[:, 0:seg] * right_prod[:, 3 * seg : 4 * seg]
        + right_prod[:, 0:seg] * left_prod[:, 3 * seg : 4 * seg]
    )


def invert_kernel(block_ref, coef_ref, work):
    base = block_ref[:PANEL, :]
    work[:, :PANEL] = 0.5 * (base + base.T)
    rows = lax.broadcasted_iota(jnp.int32, (PANEL, PANEL), 0)
    cols = lax.broadcasted_iota(jnp.int32, (PANEL, PANEL), 1)
    work[:, PANEL:] = jnp.where(rows == cols, 1.0, 0.0).astype(F32)
    row = lax.broadcasted_iota(jnp.int32, (BLOCK, 1), 0)
    brow = lax.broadcasted_iota(jnp.int32, (BLOCK, BLOCK), 0)
    bcol = lax.broadcasted_iota(jnp.int32, (BLOCK, BLOCK), 1)
    eye = jnp.where(brow == bcol, 1.0, 0.0).astype(F32)
    for b in range(PANEL // BLOCK):
        lo = b * BLOCK
        hi = lo + BLOCK
        pair = jnp.concatenate([work[lo:hi, lo:hi], eye], axis=1)
        for k in range(BLOCK):
            pivot = pair[k : k + 1, :]
            scaled = pivot / pair[k : k + 1, k : k + 1]
            factor = jnp.where(row > k, pair[:, k : k + 1], 0.0)
            pair = pair - factor * scaled
        diag = jnp.sum(pair[:, :BLOCK] * eye, axis=1, keepdims=True)
        inv = pair[:, BLOCK:] / jnp.sqrt(diag)
        done = jnp.dot(inv, work[lo:hi, :], precision=HIGH, preferred_element_type=F32)
        work[lo:hi, :] = done
        if hi < PANEL:
            lower = done[:, :PANEL]
            step = lax.dot_general(
                lower, done, (((0,), (0,)), ((), ())), precision=HIGH, preferred_element_type=F32
            )
            work[hi:, :] = work[hi:, :] - step[hi:, :]
    inverse = work[:, PANEL:]
    coef_ref[:PANEL, :] = inverse
    ahead = lax.dot_general(
        block_ref[PANEL:, :],
        inverse,
        (((1,), (1,)), ((), ())),
        precision=HIGH,
        preferred_element_type=F32,
    )
    coef_ref[PANEL:, :] = jnp.dot(ahead, inverse, precision=HIGH, preferred_element_type=F32)


def coefficients(panel_block):
    return pl.pallas_call(
        invert_kernel,
        out_shape=jax.ShapeDtypeStruct((2 * PANEL, PANEL), F32),
        in_specs=[pl.BlockSpec(memory_space=pltpu.VMEM)],
        out_specs=pl.BlockSpec(memory_space=pltpu.VMEM),
        scratch_shapes=[pltpu.VMEM((PANEL, 2 * PANEL), F32)],
        compiler_params=pltpu.CompilerParams(vmem_limit_bytes=16 * 1024 * 1024),
    )(panel_block)


def body(left_vecs, right_vecs, primal, dual_inverse, owner_map, panel_index):
    devices = lax.axis_size(("prow", "pcol"))
    grid_rows = lax.axis_size("prow")
    grid_cols = lax.axis_size("pcol")
    height = PANEL // devices
    slots = left_vecs.shape[0]
    order = left_vecs.shape[1]
    feats = primal.shape[0]
    start = panel_index[0] * PANEL
    first_slot = start // devices
    wide = lax.broadcasted_iota(jnp.int32, (devices, height, height, devices), 0)
    perm = (wide == owner_map[None, None, None, :]) & (
        lax.broadcasted_iota(jnp.int32, wide.shape, 1)
        == lax.broadcasted_iota(jnp.int32, wide.shape, 2)
    )
    perm = perm.astype(jnp.bfloat16).reshape(PANEL, PANEL)
    perm32 = perm.astype(F32)

    panel_left = lax.dynamic_slice_in_dim(left_vecs, first_slot, 2 * height, 0)
    panel_right = lax.dynamic_slice_in_dim(right_vecs, first_slot, 2 * height, 0)
    own_vecs = jnp.concatenate([panel_left, panel_right], axis=0)
    panel_vecs = lax.all_gather(own_vecs, ("prow", "pcol"), axis=0, tiled=True)
    matrices = jnp.concatenate([primal, dual_inverse], axis=0)
    raw = lax.dot_general(
        panel_vecs, matrices, (((1,), (1,)), ((), ())), preferred_element_type=F32
    )
    raw = raw.reshape(devices, 4, height, 2 * feats).transpose(1, 0, 2, 3)
    raw = raw.reshape(4, PANEL, 2, feats).astype(jnp.bfloat16)
    images = jnp.einsum("vkgf,kj->fgvj", raw, perm, preferred_element_type=F32)
    images = images.astype(jnp.bfloat16).reshape(feats, 8 * PANEL)
    piece = lax.all_gather(images, ("prow", "pcol"), axis=0, tiled=True)
    left_prod = jnp.dot(left_vecs, piece, preferred_element_type=F32)
    right_prod = jnp.dot(right_vecs, piece, preferred_element_type=F32)
    schur = combine(left_prod, right_prod)

    own_panel = lax.dynamic_slice_in_dim(schur[:, :PANEL], first_slot, 2 * height, 0)
    panel_rows = lax.all_gather(own_panel, ("prow", "pcol"), axis=0, tiled=True)
    panel_rows = panel_rows.reshape(devices, 2, height, PANEL).transpose(1, 0, 2, 3)
    panel_block = jnp.einsum(
        "kj,pkc->pjc",
        perm32,
        panel_rows.reshape(2, PANEL, PANEL),
        precision=HIGH,
        preferred_element_type=F32,
    ).reshape(2 * PANEL, PANEL)
    coef = coefficients(panel_block)

    groups = slots // (grid_rows * height)
    narrow = PANEL // grid_cols
    placed = schur.reshape(groups, grid_rows, height, 2 * PANEL).transpose(1, 2, 0, 3)
    placed = placed.reshape(slots, 2 * PANEL)
    ident = lax.broadcasted_iota(jnp.int32, (grid_rows, height, groups), 0) * height
    ident = ident + lax.broadcasted_iota(jnp.int32, ident.shape, 1)
    ident = ident + lax.broadcasted_iota(jnp.int32, ident.shape, 2) * (grid_rows * height)
    ident = ident.reshape(slots, 1)
    mixed = lax.dot_general(
        placed[:, :PANEL], coef, (((1,), (1,)), ((), ())), precision=HIGH, preferred_element_type=F32
    )
    full = jnp.where(ident >= first_slot, mixed[:, :PANEL], 0.0)
    update = jnp.where(
        ident >= first_slot + height, placed[:, PANEL:] - mixed[:, PANEL:], 0.0
    )
    both = jnp.stack(
        [
            full.reshape(grid_rows, height, groups, grid_cols, narrow),
            update.reshape(grid_rows, height, groups, grid_cols, narrow),
        ],
        axis=4,
    )
    outgoing = both.transpose(0, 3, 1, 2, 4, 5).reshape(devices, height, groups * 2 * narrow)
    arrived = lax.all_to_all(outgoing, ("prow", "pcol"), split_axis=0, concat_axis=0, tiled=True)
    final = lax.dot_general(
        arrived.reshape(PANEL, groups * 2 * narrow),
        perm32,
        (((0,), (0,)), ((), ())),
        precision=HIGH,
        preferred_element_type=F32,
    )
    final = final.reshape(groups, 2, narrow, PANEL).transpose(1, 2, 0, 3)
    final = final.reshape(2, narrow, groups * PANEL)
    return (final[0], final[1])


def solution(mesh):
    return jax.shard_map(
        body,
        mesh=mesh,
        in_specs=(
            P(("prow", "pcol"), None),
            P(("prow", "pcol"), None),
            P(("prow", "pcol"), None),
            P(("prow", "pcol"), None),
            P(),
            P(),
        ),
        out_specs=(P("pcol", "prow"), P("pcol", "prow")),
        check_vma=False,
    )
```

time: 448 us -> 398 us (0.89)
  other arithmetic: 105 us -> 8.84 us
  blocking collectives: 0 us -> 68.2 us
  local copies, waits for them, and re-layouts: 69.2 us -> 19.3 us
  Pallas kernels: 0 us -> 25.9 us
  waiting for transfers between devices: 215 us -> 227 us
    another operation x13 -> x0, other arithmetic: 57.6 us -> none  [the longest x7 34.6 us: body(): chol = jnp.linalg.cholesky(panel_block[:PANEL, :PANEL])]
    gather x7 -> x0, local copies, waits for them, and re-layouts: 45.8 us -> none  [the longest x2 35.7 us: relay_rows(): placed = jnp.take(flat, index, axis=2)]
    all_gather x0 -> x1, blocking collectives: none -> 40.3 us  [body(): panel_rows = lax.all_gather(own_panel, ('prow', 'pcol'), axis=0, tiled=True)]
    and x2 -> x0, other arithmetic: 31.3 us -> none  [the longest x1 15.7 us: relay_rows(): placed = jnp.take(flat, index, axis=2)]
    all_to_all x0 -> x1, blocking collectives: none -> 28 us  [body(): lax.all_to_all(outgoing, ('prow', 'pcol'), split_axis=0, concat_axis=0, t...]
    pallas_call x0 -> x1, Pallas kernels: none -> 25.9 us  [coefficients(): pl.pallas_call(invert_kernel, out_shape=jax.ShapeDtypeStruct((2 * PANEL,...]
    all_gather x3 -> x1, waiting for transfers between devices: 66.6 us -> 80.8 us  [body(): panel_vecs = lax.all_gather(own_vecs, ('prow', 'pcol'), axis=0, tiled=True)]
    gather x42 -> x0, other arithmetic: 11.7 us -> none  [the longest x26 7.02 us: relay_rows(): jnp.take(owner_map, within % devices) * (groups * height)]
  transfers between devices with their start and end apart: 5 -> 2, of which waited for: 4 -> 2; matrix products, arithmetic and copies ran while one was open for 34% -> 0% of each run, Pallas kernels for 0% -> 0%
where the time goes in v1:
time: 398 us
  waiting for transfers between devices  227 us (57%)
  blocking collectives  68.2 us (17%)
  matrix products  33.8 us (8%)
  Pallas kernels  25.9 us (7%)
  local copies, waits for them, and re-layouts  19.3 us (5%)
  between operations  14.9 us (4%)
  other arithmetic  8.84 us (2%)
    all_gather x1, waiting for transfers between devices, body(): piece = lax.all_gather(images, ('prow', 'pcol'), axis=0, tiled=True)  146 us
    all_gather x1, waiting for transfers between devices, body(): panel_vecs = lax.all_gather(own_vecs, ('prow', 'pcol'), axis=0, tiled=True)  80.8 us
    all_gather x1, blocking collectives, body(): panel_rows = lax.all_gather(own_panel, ('prow', 'pcol'), axis=0, tiled=True)  40.3 us
    all_to_all x1, blocking collectives, body(): lax.all_to_all(outgoing, ('prow', 'pcol'), split_axis=0, concat_axis=0, t...  28 us
    pallas_call x1, Pallas kernels, coefficients(): pl.pallas_call(invert_kernel, out_shape=jax.ShapeDtypeStruct((2 * PANEL,...  25.9 us
    dot_general x1, matrix products, body(): right_prod = jnp.dot(right_vecs, piece, preferred_element_type=F32)  13.1 us
    dot_general x1, matrix products, body(): left_prod = jnp.dot(left_vecs, piece, preferred_element_type=F32)  11.7 us
  transfers between devices with their start and end apart: 2, of which 2 were waited for; matrix products, arithmetic and copies ran while one was open for 0% of the time, Pallas kernels for 0%

profile of v1, /device:TPU:0, one launch (start us, length us, event | category | flops | bytes accessed | tf_op | source)
XLA Modules:
  0.0 397.8 jit_solution(11121179061646002787)
XLA Ops:
  7.9 1.1 constant_dynamic-slice_fusion.1
  9.0 0.7 pad_maximum_fusion
  10.0 0.7 eq.17
  10.8 80.8 %all-gather.3.cloned.1.call-done = bf16[1024,4096]{1,0:T(8,128)(2,1)} async-done(((bf16[32,4096]{1,0:T(8,128)(2,1)}), bf16[1024,4096]{1,0:T(8,128)(2,1)}) %all-gather.3.cloned.1.call-update) | async-done | bytes 8388624 | tf_op jit(solution)/shard_map/all_gather | solution.py:97
  91.6 6.3 %fusion.4 = bf16[1024,256]{1,0:T(8,128)(2,1)S(1)} fusion(bf16[1024,4096]{1,0:T(8,128)(2,1)} %all-gather.3.cloned.1.call-done, bf16[128,4096]{1,0:T(8,128)(2,1)} %param.9, bf16[128,4096]{1,0:T(8,128)(2,1)} %param.8), kind=kOutput, calls=%fused_computation.8 | convolution fusion | flops 2151940096 | bytes 11010048 | tf_op jit(solution)/shard_map/dot_general | solution.py:99
  97.9 0.1 convert_element_type.23
  98.1 0.5 fusion.7
  98.5 0.8 copy.15
  99.5 0.1 ge.30
  99.6 0.1 ge.33
  99.7 145.8 %all-gather.5.cloned.1.call-done = bf16[4096,2048]{0,1:T(8,128)(2,1)} async-done(((bf16[128,2048]{0,1:T(8,128)(2,1)}), bf16[4096,2048]{0,1:T(8,128)(2,1)}) %all-gather.5.cloned.1.call-update) | async-done | bytes 16777232 | tf_op jit(solution)/shard_map/all_gather | solution.py:106
  245.5 13.1 %convolution_bitcast_fusion = f32[512,2048]{1,0:T(8,128)S(1)} fusion(bf16[4096,2048]{0,1:T(8,128)(2,1)} %all-gather.5.cloned.1.call-done, bf16[512,4096]{1,0:T(8,128)(2,1)} %param.7), kind=kOutput, calls=%fused_computation.1 | convolution fusion | flops 8589934592 | bytes 25165824 | tf_op jit(solution)/shard_map/dot_general | solution.py:108
  258.6 11.7 %convolution_bitcast_fusion.1 = f32[512,2048]{1,0:T(8,128)S(1)} fusion(bf16[4096,2048]{0,1:T(8,128)(2,1)} %all-gather.5.cloned.1.call-done, bf16[512,4096]{1,0:T(8,128)(2,1)S(1)} %copy-done.1), kind=kOutput, calls=%fused_computation.2 | convolution fusion | flops 8589934592 | bytes 25165824 | tf_op jit(solution)/shard_map/dot_general | solution.py:107
  270.3 1.0 fusion.8
  271.4 40.3 %all_gather.11 = f32[512,256]{1,0:T(8,128)S(1)} all-gather(f32[16,256]{1,0:T(8,128)S(1)} %constant_dynamic-slice_fusion), channel_id=1, replica_groups=mesh['prow'=4,'pcol'=8] {'prow','pcol'}, dimensions={0}, use_global_device_ids=true | all-gather | bytes 540672 | tf_op jit(solution)/shard_map/all_gather | solution.py:112
  311.6 0.5 fusion.14
  312.2 25.9 %shard_map.77 = f32[512,256]{1,0:T(8,128)S(1)} custom-call(f32[512,256]{1,0:T(8,128)S(1)} %bitcast.61), custom_call_target="tpu_custom_call" | custom-call | tf_op jit(solution)/shard_map/pallas_call | solution.py:66
  338.1 0.6 copy.16
  338.7 1.0 fusion.12
  339.8 0.2 slice_select_fusion
  340.0 0.5 stack_reshape.6
  340.5 3.9 copy.19
  344.4 0.5 stack_reshape.7
  344.9 2.2 copy.20
  347.1 6.8 %maximum_bitcast_fusion = f32[4,8,8,16,2,32]{5,4,3,2,1,0:T(2,128)} fusion(f32[4,8,16,8,1,32]{5,4,2,1,3,0:T(1,128)S(1)} %copy.20, f32[4,8,16,8,1,32]{5,4,2,1,3,0:T(1,128)S(1)} %copy-done), kind=kLoop, calls=%fused_computation | loop fusion | flops 262144 | bytes 2097152 | tf_op jit(solution)/shard_map/transpose | solution.py:145
  353.8 6.2 %reshape.95 = f32[32,8,1024]{2,1,0:T(8,128)S(1)} reshape(f32[4,8,8,16,2,32]{5,4,3,2,1,0:T(2,128)} %maximum_bitcast_fusion) | data formatting | bytes 2097152 | tf_op jit(solution)/shard_map/reshape | solution.py:145
  360.1 28.0 %all_to_all.5 = f32[32,8,1024]{2,1,0:T(8,128)S(1)} all-to-all(f32[32,8,1024]{2,1,0:T(8,128)S(1)} %reshape.95), channel_id=1, replica_groups=mesh['prow'=4,'pcol'=8] {'prow','pcol'}, dimensions={0} | all-to-all | bytes 2097152 | tf_op jit(solution)/shard_map/all_to_all | solution.py:146
  388.1 0.3 copy.21
  388.4 0.7 convolution_bitcast_fusion.2
  389.1 0.1 fusion.36
  389.2 0.8 copy.29
  390.1 0.8 copy.30
  (21 shorter events, 0.6 us)
Async XLA Ops:
  7.2 84.5 %all-gather.3.cloned.1.call-start = ((), (), s32[]{:S(2)}) async-start(), calls=%async_computation.1 | async-start | bytes 8650752 | tf_op jit(solution)/shard_map/all_gather | solution.py:97
  9.7 235.7 %all-gather.5.cloned.1.call-start = ((), (), s32[]{:S(2)}) async-start(), calls=%async_computation.2 | async-start | bytes 17301504 | tf_op jit(solution)/shard_map/all_gather | solution.py:106
  245.4 13.1 %copy-start.1 = (bf16[512,4096]{1,0:T(8,128)(2,1)S(1)}, bf16[512,4096]{1,0:T(8,128)(2,1)}, u32[]{:S(2)}) copy-start(bf16[512,4096]{1,0:T(8,128)(2,1)} %param.6) | copy-start | bytes 12582916
  344.9 2.2 copy-start
Sparse Core Ops, SparseCore 0:
  11.4 80.1 all-gather.2
  99.5 145.8 all-gather.4
